TPU v7x, 128 devices: a whole 4x4x4 slice. The times are simulated.
128 devices in a mesh: dp: 16 (over y, x), expert: 8 (over z, core).
Axes of the slice: x: 4, y: 4, z: 4, core: 2. Of those that a mesh axis runs over, the one named last changes fastest.
Arguments:
- tokens: bfloat16 [16384, 1280], P(('dp', 'expert')), may hold values from -6 to 6
- cotangent: bfloat16 [16384, 1280], P(('dp', 'expert')), may hold values from -4 to 4
- gate_weights: float32 [16384, 2], P(('dp', 'expert')), may hold values from 0.1 to 1
- expert_ids: int32 [16384, 2], P(('dp', 'expert')), may hold values from 0 to 15, as said below
- segments: int32 [128, 128], P(('dp', 'expert')), may hold values from 0 to 3, never falling along the last dimension, each value on 1 to 64 neighbouring positions
- keep_counts: int32 [128, 4], P(('dp', 'expert')), may hold values from 1 to 64
- expand_weight: bfloat16 [16, 2560, 1280], P('expert', 'dp'), may hold values from -0.15625 to 0.15625
- reduce_weight: bfloat16 [16, 2560, 1280], P('expert', 'dp'), may hold values from -0.125 to 0.125
Outputs:
- output: bfloat16 [16384, 1280], P(('dp', 'expert'))
- tokens_grad: bfloat16 [16384, 1280], P(('dp', 'expert'))
- gating_grad: float32 [16384, 2], P(('dp', 'expert'))
- expand_grad: bfloat16 [16, 2560, 1280], P('expert', 'dp')
- reduce_grad: bfloat16 [16, 2560, 1280], P('expert', 'dp')
Inputs may be any that keep to these rules, and one draw needn't show every extreme that they name: `expert_ids`: the 128 tokens of one sequence name each expert exactly 16 times, and a token's 2 experts differ. `segments`: within a sequence the ids never fall, every image 0 to 3 appears, each holds 1 to 64 positions.
All inputs are finite; a program needn't handle non-finite values.
Results may differ from a plain program's by a relative error of at most 0.015.
Values may be sent and summed in bfloat16 or wider, within the bound.
A program may use at most 128 MiB of HBM per device.

v0:
```python
import jax
import jax.numpy as jnp
from jax import lax
from jax.sharding import PartitionSpec as P

epsilon = 1e-06
root_half = 0.7071067811865476
density_scale = 0.3989422804014327


def gelu_value(values):
    return 0.5 * values * (1.0 + jax.scipy.special.erf(values * root_half))


def gelu_slope(values):
    return (
        0.5 * (1.0 + jax.scipy.special.erf(values * root_half))
        + values * jnp.exp(-0.5 * values * values) * density_scale
    )


def project_up(rows, weight):
    return jnp.einsum("rld,lhd->rlh", rows, weight, preferred_element_type=jnp.float32)


def project_down(hidden, weight):
    return jnp.einsum("rlh,lhd->rld", hidden, weight, preferred_element_type=jnp.float32)


def outer_rows(left, right):
    return jnp.einsum("rlh,rld->lhd", left, right, preferred_element_type=jnp.float32)


def body(
    tokens, cotangent, gate_weights, expert_ids, segments, keep_counts, expand_weight, reduce_weight
):
    tok_count = tokens.shape[0]
    top_count = expert_ids.shape[1]
    width = tokens.shape[1]
    sources = lax.axis_size("expert")
    local = expand_weight.shape[0]
    total_experts = local * sources
    pick_count = top_count * tok_count
    capacity = pick_count // total_experts
    image_ids = segments[0]
    position = jnp.arange(tok_count, dtype=jnp.int32)
    earlier_img = jnp.sum((image_ids[None, :] < image_ids[:, None]).astype(jnp.int32), axis=1)
    image_match = (
        image_ids[:, None] == jnp.arange(keep_counts.shape[1], dtype=jnp.int32)[None, :]
    ).astype(jnp.int32)
    keep_token = jnp.sum(image_match * keep_counts, axis=1)
    alive = (position - earlier_img < keep_token).astype(jnp.float32)
    tokens_wide = tokens.astype(jnp.float32)
    mean_rows = jnp.mean(tokens_wide, axis=1, keepdims=True)
    centred = tokens_wide - mean_rows
    inv_scale = lax.rsqrt(jnp.mean(centred * centred, axis=1, keepdims=True) + epsilon)
    normed = centred * inv_scale
    normed_low = normed.astype(jnp.bfloat16)
    choice_list = expert_ids.reshape(-1)
    matches = (choice_list[:, None] == jnp.arange(total_experts, dtype=jnp.int32)[None, :]).astype(
        jnp.int32
    )
    before = jnp.cumsum(matches, axis=0) - matches
    slot_list = jnp.sum(before * matches, axis=1)
    target = choice_list * capacity + slot_list
    order = (
        jnp.zeros((pick_count,), jnp.int32).at[target].set(jnp.arange(pick_count, dtype=jnp.int32))
    )
    source = order // top_count
    alive_pick = jnp.repeat(alive, top_count)
    weight_pick = gate_weights.reshape(-1) * alive_pick
    sent_rows = jnp.where(
        alive_pick[order][:, None] > 0, normed_low[source], jnp.zeros((), jnp.bfloat16)
    )
    cot_wide = cotangent.astype(jnp.float32)
    sent_grads = (cot_wide[source] * weight_pick[order][:, None]).astype(jnp.bfloat16)

    def to_slots(flat):
        return (
            flat.reshape(sources, local, capacity, width)
            .transpose(0, 2, 1, 3)
            .reshape(sources * capacity, local, width)
        )

    def from_slots(rows):
        return (
            rows.reshape(sources, capacity, local, width)
            .transpose(0, 2, 1, 3)
            .reshape(pick_count, width)
        )

    arrived = to_slots(lax.all_to_all(sent_rows, "expert", split_axis=0, concat_axis=0, tiled=True))
    arrived_grads = to_slots(
        lax.all_to_all(sent_grads, "expert", split_axis=0, concat_axis=0, tiled=True)
    )
    slot_rows = arrived.shape[0]
    all_rows = lax.all_gather(arrived, "dp", axis=0, tiled=True)
    pre = project_up(all_rows, expand_weight)
    hidden = gelu_value(pre).astype(jnp.bfloat16)
    results = lax.psum_scatter(
        project_down(hidden, reduce_weight).astype(jnp.bfloat16),
        "dp",
        scatter_dimension=0,
        tiled=True,
    )
    all_grads = lax.all_gather(arrived_grads, "dp", axis=0, tiled=True)
    back_hidden = project_up(all_grads, reduce_weight)
    dpre = (back_hidden * gelu_slope(pre)).astype(jnp.bfloat16)
    input_rows = lax.psum_scatter(
        project_down(dpre, expand_weight).astype(jnp.bfloat16),
        "dp",
        scatter_dimension=0,
        tiled=True,
    )

    def add_block(block, totals):
        offset = block * slot_rows
        hidden_block = lax.dynamic_slice_in_dim(hidden, offset, slot_rows, 0)
        dpre_block = lax.dynamic_slice_in_dim(dpre, offset, slot_rows, 0)
        grad_block = lax.dynamic_slice_in_dim(all_grads, offset, slot_rows, 0)
        row_block = lax.dynamic_slice_in_dim(all_rows, offset, slot_rows, 0)
        second_piece = lax.optimization_barrier(
            outer_rows(hidden_block, grad_block).astype(jnp.bfloat16)
        ).astype(jnp.float32)
        first_piece = lax.optimization_barrier(
            outer_rows(dpre_block, row_block).astype(jnp.bfloat16)
        ).astype(jnp.float32)
        return (totals[0] + first_piece, totals[1] + second_piece)

    empty = jnp.zeros(expand_weight.shape, jnp.float32)
    first_total, second_total = lax.fori_loop(
        0, all_rows.shape[0] // slot_rows, add_block, (empty, empty)
    )
    expand_grad = first_total.astype(jnp.bfloat16)
    reduce_grad = second_total.astype(jnp.bfloat16)
    returned = lax.all_to_all(
        from_slots(results), "expert", split_axis=0, concat_axis=0, tiled=True
    )
    result_pick = returned[target].astype(jnp.float32).reshape(tok_count, top_count, -1)
    output = (
        tokens_wide + jnp.sum(result_pick * weight_pick.reshape(tok_count, top_count, 1), axis=1)
    ).astype(jnp.bfloat16)
    gating_grad = alive_pick.reshape(tok_count, top_count) * jnp.sum(
        cot_wide[:, None, :] * result_pick, axis=2
    )
    returned_grads = lax.all_to_all(
        from_slots(input_rows), "expert", split_axis=0, concat_axis=0, tiled=True
    )
    input_pick = returned_grads[target].astype(jnp.float32).reshape(tok_count, top_count, -1)
    grad_norm = jnp.sum(input_pick * alive_pick.reshape(tok_count, top_count, 1), axis=1)
    tokens_grad = cot_wide + inv_scale * (
        grad_norm
        - jnp.mean(grad_norm, axis=1, keepdims=True)
        - normed * jnp.mean(grad_norm * normed, axis=1, keepdims=True)
    )
    return (output, tokens_grad.astype(jnp.bfloat16), gating_grad, expand_grad, reduce_grad)


def solution(mesh):
    in_specs = (
        P(("dp", "expert"), None),
        P(("dp", "expert"), None),
        P(("dp", "expert"), None),
        P(("dp", "expert"), None),
        P(("dp", "expert"), None),
        P(("dp", "expert"), None),
        P("expert", "dp", None),
        P("expert", "dp", None),
    )
    out_specs = (
        P(("dp", "expert"), None),
        P(("dp", "expert"), None),
        P(("dp", "expert"), None),
        P("expert", "dp", None),
        P("expert", "dp", None),
    )
    return jax.shard_map(body, mesh=mesh, in_specs=in_specs, out_specs=out_specs, check_vma=False)
```

profile of v0, /device:TPU:1, one launch (start us, length us, event | category | flops | bytes accessed | tf_op | source)
XLA Modules:
  0.0 434.9 jit_solution(15564184737724795476)
XLA Ops:
  16.0 1.9 gather_fusion
  19.6 17.6 %all_to_all.36 = bf16[8,32,1280]{2,1,0:T(8,128)(2,1)S(1)} all-to-all(bf16[8,32,1280]{2,1,0:T(8,128)(2,1)S(1)} %broadcast_select_fusion), channel_id=1, replica_groups=mesh['dp'=16,'expert'=8] {'expert'}, dimensions={0} | all-to-all | bytes 1310720 | tf_op jit(solution)/shard_map/all_to_all | solution.py:92
  38.4 1.9 gather_fusion.4
  41.9 14.2 %all_to_all.37 = bf16[8,32,1280]{2,1,0:T(8,128)(2,1)S(1)} all-to-all(bf16[8,32,1280]{2,1,0:T(8,128)(2,1)S(1)} %multiply_convert_fusion.1), channel_id=1, replica_groups=mesh['dp'=16,'expert'=8] {'expert'}, dimensions={0} | all-to-all | bytes 1310720 | tf_op jit(solution)/shard_map/all_to_all | solution.py:94
  57.1 61.1 %all-gather.3.cloned.1.call-done = bf16[2048,2,1280]{2,0,1:T(8,128)(2,1)} async-done(((bf16[128,2,1280]{2,0,1:T(8,128)(2,1)}), bf16[2048,2,1280]{2,0,1:T(8,128)(2,1)}) %all-gather.3.cloned.1.call-update) | async-done | bytes 10485776 | tf_op jit(solution)/shard_map/all_gather | solution.py:97
  118.2 9.1 %multiply_convert_fusion = (bf16[2048,2,160]{0,2,1:T(8,128)(2,1)S(1)}, f32[2048,2,160]{0,2,1:T(8,128)}) fusion(bf16[2048,2,1280]{2,0,1:T(8,128)(2,1)} %all-gather.3.cloned.1.call-done, bf16[2,160,1280]{2,1,0:T(8,128)(2,1)S(1)} %copy-done), kind=kOutput, calls=%fused_computation.30 | convolution fusion | flops 1680998400 | bytes 15237120 | tf_op jit(solution)/shard_map/rld,lhd->rlh/dot_general | solution.py:23
  127.3 73.6 %all-gather.5.cloned.1.call-done = bf16[2048,2,1280]{2,0,1:T(8,128)(2,1)} async-done(((bf16[128,2,1280]{2,0,1:T(8,128)(2,1)}), bf16[2048,2,1280]{2,0,1:T(8,128)(2,1)}) %all-gather.5.cloned.1.call-update) | async-done | bytes 10485776 | tf_op jit(solution)/shard_map/all_gather | solution.py:106
  200.9 8.6 %fusion.9 = bf16[2048,2,160]{0,2,1:T(8,128)(2,1)S(1)} fusion(bf16[2048,2,1280]{2,0,1:T(8,128)(2,1)} %all-gather.5.cloned.1.call-done, bf16[2,160,1280]{2,1,0:T(8,128)(2,1)} %param.17, f32[2048,2,160]{0,2,1:T(8,128)} %get-tuple-element.189), kind=kOutput, calls=%fused_computation.25 | convolution fusion | flops 1684275200 | bytes 15237120 | tf_op jit(solution)/shard_map/rld,lhd->rlh/dot_general | solution.py:23
  210.6 5.6 %fusion.7 = bf16[2048,2,1280]{2,0,1:T(8,128)(2,1)} fusion(bf16[2048,2,160]{0,2,1:T(8,128)(2,1)S(1)} %fusion.9, bf16[2,160,1280]{2,1,0:T(8,128)(2,1)S(1)} %copy-done), kind=kOutput, calls=%fused_computation.20 | convolution fusion | flops 1682964480 | bytes 12615680 | tf_op jit(solution)/shard_map/rlh,lhd->rld/dot_general | solution.py:27
  217.3 5.7 %fusion.6 = bf16[2048,2,1280]{2,0,1:T(8,128)(2,1)} fusion(bf16[2048,2,160]{0,2,1:T(8,128)(2,1)S(1)} %get-tuple-element.244, bf16[2,160,1280]{2,1,0:T(8,128)(2,1)S(1)} %copy-done.10), kind=kOutput, calls=%fused_computation.19 | convolution fusion | flops 1682964480 | bytes 12615680 | tf_op jit(solution)/shard_map/rlh,lhd->rld/dot_general | solution.py:27
  223.1 81.8 %reduce-scatter.5.cloned.1.call-done = bf16[128,2,1280]{2,0,1:T(8,128)(2,1)} async-done(((bf16[2048,2,1280]{2,0,1:T(8,128)(2,1)}), bf16[128,2,1280]{2,0,1:T(8,128)(2,1)}) %reduce-scatter.5.cloned.1.call-update) | async-done | bytes 655376 | tf_op jit(solution)/shard_map/reduce_scatter | solution.py:109
  304.9 2.0 copy.47
  306.9 5.9 %all-to-all-start.3 = ((bf16[8,32,1280]{2,1,0:T(8,128)(2,1)}), bf16[8,32,1280]{2,1,0:T(8,128)(2,1)}, u32[]{:S(2)}, u32[]{:S(2)}) async-start(bf16[8,32,1280]{2,1,0:T(8,128)(2,1)} %bitcast.23), calls=%async_computation.5 | async-start | bytes 1310720 | tf_op jit(solution)/shard_map/all_to_all | solution.py:146
  312.8 86.8 %while.16 = (s32[]{:T(128)}, f32[2,160,1280]{2,1,0:T(8,128)}, f32[2,160,1280]{2,1,0:T(8,128)S(1)}, bf16[2048,2,160]{0,2,1:T(8,128)(2,1)}, bf16[2048,2,1280]{2,0,...) while((s32[]{:T(128)}, f32[2,160,1280]{2,1,0:T(8,128)}, ...), condition=%wide.region_17.18_spmd.clone, body=%wide.region_16.17_spmd.clone.sunk | while | flops 212992000 | bytes 24414436 | solution.py:131
  318.2 1.6 convolution_convert_fusion.6
  323.6 1.6 convolution_convert_fusion.6
  329.1 1.6 convolution_convert_fusion.6
  334.6 1.6 convolution_convert_fusion.6
  340.0 1.6 convolution_convert_fusion.6
  350.9 1.6 convolution_convert_fusion.6
  361.8 1.6 convolution_convert_fusion.6
  367.2 1.6 convolution_convert_fusion.6
  388.8 1.6 convolution_convert_fusion.6
  394.2 1.6 convolution_convert_fusion.6
  402.3 2.0 copy.42
  404.3 4.8 %all-to-all-start.1 = ((bf16[8,32,1280]{2,1,0:T(8,128)(2,1)}), bf16[8,32,1280]{2,1,0:T(8,128)(2,1)S(1)}, u32[]{:S(2)}, u32[]{:S(2)}) async-start(bf16[8,32,1280]{2,1,0:T(8,128)(2,1)} %bitcast.13), calls=%async_computation.2 | async-start | bytes 1310720 | tf_op jit(solution)/shard_map/all_to_all | solution.py:136
  409.1 2.9 gather_fusion.5
  412.4 1.7 reshape.174
  414.2 3.0 multiply_reduce_fusion.2
  417.6 2.5 all-to-all-done.1
  421.3 1.7 reshape.173
  423.0 3.5 multiply_reduce_fusion
  (189 shorter events, 93.0 us)
Async XLA Ops:
  7.2 111.0 %copy-start = (bf16[2,160,1280]{2,1,0:T(8,128)(2,1)S(1)}, bf16[2,160,1280]{2,1,0:T(8,128)(2,1)}, u32[]{:S(2)}) copy-start(bf16[2,160,1280]{2,1,0:T(8,128)(2,1)} %param.16) | copy-start | bytes 2457604
  7.2 10.8 %copy-start.5 = (bf16[128,1280]{1,0:T(8,128)(2,1)S(1)}, bf16[128,1280]{1,0:T(8,128)(2,1)}, u32[]{:S(2)}) copy-start(bf16[128,1280]{1,0:T(8,128)(2,1)} %param.10) | copy-start | bytes 983044
  7.2 111.0 %all-gather.3.cloned.1.call-start = ((), (), s32[]{:S(2)}) async-start(), calls=%async_computation.6 | async-start | bytes 11141120 | tf_op jit(solution)/shard_map/all_gather | solution.py:97
  19.6 18.5 %copy-start.11 = (f32[128,2]{0,1:T(2,128)S(1)}, f32[128,2]{0,1:T(2,128)}, u32[]{:S(2)}) copy-start(f32[128,2]{0,1:T(2,128)} %param.12) | copy-start | bytes 3076
  37.2 3.3 copy-start.8
  38.1 162.8 %all-gather.5.cloned.1.call-start = ((), (), s32[]{:S(2)}) async-start(), calls=%async_computation.8 | async-start | bytes 11141120 | tf_op jit(solution)/shard_map/all_gather | solution.py:106
  57.0 247.9 %reduce-scatter.5.cloned.1.call-start = ((), (), s32[]{:S(2)}) async-start(), calls=%async_computation.9 | async-start | bytes 11141120 | tf_op jit(solution)/shard_map/reduce_scatter | solution.py:109
  127.3 89.1 %copy-start.6 = (bf16[2048,2,160]{0,2,1:T(8,128)(2,1)}, bf16[2048,2,160]{0,2,1:T(8,128)(2,1)S(1)}, u32[]{:S(2)}) copy-start(bf16[2048,2,160]{0,2,1:T(8,128)(2,1)S(1)} %get-tuple-element.244) | copy-start | bytes 3932164
  216.2 186.2 %reduce-scatter.3.cloned.1.call-start = ((), (), s32[]{:S(2)}) async-start(), calls=%async_computation.7 | async-start | bytes 11141120 | tf_op jit(solution)/shard_map/reduce_scatter | solution.py:100
  306.9 97.5 %all-to-all-start.3 = ((bf16[8,32,1280]{2,1,0:T(8,128)(2,1)}), bf16[8,32,1280]{2,1,0:T(8,128)(2,1)}, u32[]{:S(2)}, u32[]{:S(2)}) async-start(bf16[8,32,1280]{2,1,0:T(8,128)(2,1)} %bitcast.23), calls=%async_computation.5 | async-start | bytes 1310720 | tf_op jit(solution)/shard_map/all_to_all | solution.py:146
  312.8 3.1 copy-start.2
  317.0 1.2 copy-start.3
  318.2 3.1 copy-start.2
  322.5 1.2 copy-start.3
  323.6 3.2 copy-start.2
  329.1 3.2 copy-start.2
  334.6 3.2 copy-start.2
  340.0 3.2 copy-start.2
  345.5 3.1 copy-start.2
  350.9 3.1 copy-start.2
  356.3 3.1 copy-start.2
  361.8 3.1 copy-start.2
  367.2 3.1 copy-start.2
  372.6 3.1 copy-start.2
  378.0 3.1 copy-start.2
  383.4 3.1 copy-start.2
  388.8 3.2 copy-start.2
  394.2 3.2 copy-start.2
  399.6 1.7 copy-start.4
  404.3 15.7 %all-to-all-start.1 = ((bf16[8,32,1280]{2,1,0:T(8,128)(2,1)}), bf16[8,32,1280]{2,1,0:T(8,128)(2,1)S(1)}, u32[]{:S(2)}, u32[]{:S(2)}) async-start(bf16[8,32,1280]{2,1,0:T(8,128)(2,1)} %bitcast.13), calls=%async_computation.2 | async-start | bytes 1310720 | tf_op jit(solution)/shard_map/all_to_all | solution.py:136
  423.0 4.2 copy-start.9
  423.0 5.4 %copy-start.1 = (bf16[2,160,1280]{2,1,0:T(8,128)(2,1)S(1)}, bf16[2,160,1280]{2,1,0:T(8,128)(2,1)}, u32[]{:S(2)}) copy-start(bf16[2,160,1280]{2,1,0:T(8,128)(2,1)} %param.16) | copy-start | bytes 2457604
  (16 other events, 18.8 us)
Sparse Core Ops, SparseCore 0:
  38.2 79.9 all-gather.2
  120.9 79.9 all-gather.4
  216.3 88.5 reduce-scatter.4
  308.2 88.6 reduce-scatter.2
where the time goes:
time: 436 us; the launch traced here: 435 us
  waiting for transfers between devices  219 us (50%)
  matrix products  79 us (18%)
  local copies, waits for them, and re-layouts  45.8 us (11%)
  other arithmetic  33.5 us (8%)
  blocking collectives  31.8 us (7%)
  between operations  14 us (3%)
  starting transfers between devices  11.1 us (3%)
    reduce_scatter x1, waiting for transfers between devices, body(): lax.psum_scatter(project_down(dpre, expand_weight).astype(jnp.bfloat16),...  81.8 us
    all_gather x1, waiting for transfers between devices, body(): all_grads = lax.all_gather(arrived_grads, 'dp', axis=0, tiled=True)  73.6 us
    all_gather x1, waiting for transfers between devices, body(): all_rows = lax.all_gather(arrived, 'dp', axis=0, tiled=True)  61.1 us
    dot_general x32, matrix products, outer_rows(): jnp.einsum('rlh,rld->lhd', left, right, preferred_element_type=jnp.float32)  50.1 us
    while x64, local copies, waits for them, and re-layouts  19 us
    dot_general x2, matrix products, project_up(): jnp.einsum('rld,lhd->rlh', rows, weight, preferred_element_type=jnp.float32)  17.7 us
    all_to_all x1, blocking collectives, body(): lax.all_to_all(sent_rows, 'expert', split_axis=0, concat_axis=0, tiled=True)  17.6 us
    add x16, other arithmetic, add_block(): return (totals[0] + first_piece, totals[1] + second_piece)  17.2 us
  transfers between devices with their start and end apart: 6, of which 4 were waited for; matrix products, arithmetic and copies ran while one was open for 23% of the time, Pallas kernels for 0%

commit v1 on v0

--- a/solution.py
+++ b/solution.py
@@ -94,7 +94,13 @@
         lax.all_to_all(sent_grads, "expert", split_axis=0, concat_axis=0, tiled=True)
     )
     slot_rows = arrived.shape[0]
-    all_rows = lax.all_gather(arrived, "dp", axis=0, tiled=True)
+    size = lax.axis_size("dp")
+    moving, shards = (arrived, [arrived])
+    for _ in range(size - 1):
+        moving = lax.ppermute(moving, "dp", [(i, (i + 1) % size) for i in range(size)])
+        shards.insert(0, moving)
+    line = jnp.concatenate(shards, axis=0)
+    all_rows = jnp.roll(line, (lax.axis_index("dp") + 1) * arrived.shape[0], axis=0)
     pre = project_up(all_rows, expand_weight)
     hidden = gelu_value(pre).astype(jnp.bfloat16)
     results = lax.psum_scatter(

time: 436 us -> 760 us (1.74)
  waiting for transfers between devices: 219 us -> 470 us
  other arithmetic: 33.5 us -> 85.4 us
  local copies, waits for them, and re-layouts: 45.8 us -> 86.4 us
  blocking collectives: 31.8 us -> 0 us
  starting transfers between devices: 11.1 us -> 25.1 us
    ppermute x0 -> x15, waiting for transfers between devices: none -> 277 us  [body(): lax.ppermute(moving, 'dp', [(i, (i + 1) % size) for i in range(size)])]
    reduce_scatter x1, waiting for transfers between devices: 0.01 us -> 92.9 us  [body(): lax.psum_scatter(project_down(hidden, reduce_weight).astype(jnp.bfloat16)...]
    all_gather x1, waiting for transfers between devices: 73.6 us -> 0.02 us  [body(): all_grads = lax.all_gather(arrived_grads, 'dp', axis=0, tiled=True)]
    all_gather x1 -> x0, waiting for transfers between devices: 61.1 us -> none  [body(): all_rows = lax.all_gather(arrived, 'dp', axis=0, tiled=True)]
    unnamed x23 -> x96, local copies, waits for them, and re-layouts: 4.25 us -> 52.3 us
    add x16, other arithmetic: 17.2 us -> 64.3 us  [add_block(): return (totals[0] + first_piece, totals[1] + second_piece)]
    all_to_all x2 -> x0, blocking collectives: 31.8 us -> none  [the longest x1 17.6 us: body(): lax.all_to_all(sent_rows, 'expert', split_axis=0, concat_axis=0, tiled=True)]
    while x64 -> x0, local copies, waits for them, and re-layouts: 19 us -> none
  transfers between devices with their start and end apart: 6 -> 22, of which waited for: 4 -> 19; matrix products, arithmetic and copies ran while one was open for 23% -> 28% of each run, Pallas kernels for 0% -> 0%
where the time goes in v1:
time: 760 us; the launch traced here: 758 us
  waiting for transfers between devices  470 us (62%)
  local copies, waits for them, and re-layouts  86.4 us (11%)
  other arithmetic  85.4 us (11%)
  matrix products  76.6 us (10%)
  starting transfers between devices  25.1 us (3%)
  between operations  14.1 us (2%)
    ppermute x15, waiting for transfers between devices, body(): lax.ppermute(moving, 'dp', [(i, (i + 1) % size) for i in range(size)])  277 us
    reduce_scatter x1, waiting for transfers between devices, body(): lax.psum_scatter(project_down(hidden, reduce_weight).astype(jnp.bfloat16)...  92.9 us
    reduce_scatter x1, waiting for transfers between devices, body(): lax.psum_scatter(project_down(dpre, expand_weight).astype(jnp.bfloat16),...  84.2 us
    add x16, other arithmetic, add_block(): return (totals[0] + first_piece, totals[1] + second_piece)  64.3 us
    unnamed x96, local copies, waits for them, and re-layouts  52.3 us
    dot_general x32, matrix products, outer_rows(): jnp.einsum('rlh,rld->lhd', left, right, preferred_element_type=jnp.float32)  47.9 us
    dot_general x2, matrix products, project_up(): jnp.einsum('rld,lhd->rlh', rows, weight, preferred_element_type=jnp.float32)  17.5 us
  transfers between devices with their start and end apart: 22, of which 19 were waited for; matrix products, arithmetic and copies ran while one was open for 28% of the time, Pallas kernels for 0%

profile of v1, /device:TPU:1, one launch (start us, length us, event | category | flops | bytes accessed | tf_op | source)
XLA Modules:
  0.0 758.1 jit_solution(3646927416570607789)
XLA Ops:
  21.3 6.8 all-to-all-start
  32.7 6.3 all-to-all-done
  39.0 4.9 all-to-all-start.2
  45.3 9.7 %all-to-all-done.2 = bf16[8,32,1280]{2,1,0:T(8,128)(2,1)} async-done(((bf16[8,32,1280]{2,1,0:T(8,128)(2,1)}), bf16[8,32,1280]{2,1,0:T(8,128)(2,1)}, u32[]{:S(2)}, u32[]{:S(2)}) %all-to-all-start.2) | async-done | bytes 655392 | tf_op jit(solution)/shard_map/all_to_all | solution.py:94
  57.0 6.9 collective-permute-done
  63.9 28.0 %collective-permute-done.1 = bf16[128,2,1280]{2,0,1:T(8,128)(2,1)S(1)} collective-permute-done((bf16[128,2,1280]{2,0,1:T(8,128)(2,1)S(1)}, bf16[128,2,1280]{2,0,1:T(8,128)(2,1)S(1)}, u32[]{:S(2)}, u32[]{:S(2)}) %collective-permute-start.1) | collective-permute-done | bytes 655392 | tf_op jit(solution)/shard_map/ppermute | solution.py:100
  91.9 21.0 %collective-permute-done.2 = bf16[128,2,1280]{2,0,1:T(8,128)(2,1)S(1)} collective-permute-done((bf16[128,2,1280]{2,0,1:T(8,128)(2,1)S(1)}, bf16[128,2,1280]{2,0,1:T(8,128)(2,1)S(1)}, u32[]{:S(2)}, u32[]{:S(2)}) %collective-permute-start.2) | collective-permute-done | bytes 655392 | tf_op jit(solution)/shard_map/ppermute | solution.py:100
  113.8 31.5 %collective-permute-done.3 = bf16[128,2,1280]{2,0,1:T(8,128)(2,1)S(1)} collective-permute-done((bf16[128,2,1280]{2,0,1:T(8,128)(2,1)S(1)}, bf16[128,2,1280]{2,0,1:T(8,128)(2,1)S(1)}, u32[]{:S(2)}, u32[]{:S(2)}) %collective-permute-start.3) | collective-permute-done | bytes 655392 | tf_op jit(solution)/shard_map/ppermute | solution.py:100
  146.2 31.5 %collective-permute-done.4 = bf16[128,2,1280]{2,0,1:T(8,128)(2,1)S(1)} collective-permute-done((bf16[128,2,1280]{2,0,1:T(8,128)(2,1)S(1)}, bf16[128,2,1280]{2,0,1:T(8,128)(2,1)S(1)}, u32[]{:S(2)}, u32[]{:S(2)}) %collective-permute-start.4) | collective-permute-done | bytes 655392 | tf_op jit(solution)/shard_map/ppermute | solution.py:100
  178.5 14.6 %collective-permute-done.5 = bf16[128,2,1280]{2,0,1:T(8,128)(2,1)S(1)} collective-permute-done((bf16[128,2,1280]{2,0,1:T(8,128)(2,1)S(1)}, bf16[128,2,1280]{2,0,1:T(8,128)(2,1)S(1)}, u32[]{:S(2)}, u32[]{:S(2)}) %collective-permute-start.5) | collective-permute-done | bytes 655392 | tf_op jit(solution)/shard_map/ppermute | solution.py:100
  194.0 13.7 %collective-permute-done.6 = bf16[128,2,1280]{2,0,1:T(8,128)(2,1)S(1)} collective-permute-done((bf16[128,2,1280]{2,0,1:T(8,128)(2,1)S(1)}, bf16[128,2,1280]{2,0,1:T(8,128)(2,1)S(1)}, u32[]{:S(2)}, u32[]{:S(2)}) %collective-permute-start.6) | collective-permute-done | bytes 655392 | tf_op jit(solution)/shard_map/ppermute | solution.py:100
  208.5 12.8 %collective-permute-done.7 = bf16[128,2,1280]{2,0,1:T(8,128)(2,1)S(1)} collective-permute-done((bf16[128,2,1280]{2,0,1:T(8,128)(2,1)S(1)}, bf16[128,2,1280]{2,0,1:T(8,128)(2,1)S(1)}, u32[]{:S(2)}, u32[]{:S(2)}) %collective-permute-start.7) | collective-permute-done | bytes 655392 | tf_op jit(solution)/shard_map/ppermute | solution.py:100
  222.1 13.4 %collective-permute-done.8 = bf16[128,2,1280]{2,0,1:T(8,128)(2,1)S(1)} collective-permute-done((bf16[128,2,1280]{2,0,1:T(8,128)(2,1)S(1)}, bf16[128,2,1280]{2,0,1:T(8,128)(2,1)S(1)}, u32[]{:S(2)}, u32[]{:S(2)}) %collective-permute-start.8) | collective-permute-done | bytes 655392 | tf_op jit(solution)/shard_map/ppermute | solution.py:100
  236.4 14.5 %collective-permute-done.9 = bf16[128,2,1280]{2,0,1:T(8,128)(2,1)S(1)} collective-permute-done((bf16[128,2,1280]{2,0,1:T(8,128)(2,1)S(1)}, bf16[128,2,1280]{2,0,1:T(8,128)(2,1)S(1)}, u32[]{:S(2)}, u32[]{:S(2)}) %collective-permute-start.9) | collective-permute-done | bytes 655392 | tf_op jit(solution)/shard_map/ppermute | solution.py:100
  251.7 15.6 %collective-permute-done.10 = bf16[128,2,1280]{2,0,1:T(8,128)(2,1)S(1)} collective-permute-done((bf16[128,2,1280]{2,0,1:T(8,128)(2,1)S(1)}, bf16[128,2,1280]{2,0,1:T(8,128)(2,1)S(1)}, u32[]{:S(2)}, u32[]{:S(2)}) %collective-permute-start.10) | collective-permute-done | bytes 655392 | tf_op jit(solution)/shard_map/ppermute | solution.py:100
  268.1 19.8 %collective-permute-done.11 = bf16[128,2,1280]{2,0,1:T(8,128)(2,1)S(1)} collective-permute-done((bf16[128,2,1280]{2,0,1:T(8,128)(2,1)S(1)}, bf16[128,2,1280]{2,0,1:T(8,128)(2,1)S(1)}, u32[]{:S(2)}, u32[]{:S(2)}) %collective-permute-start.11) | collective-permute-done | bytes 655392 | tf_op jit(solution)/shard_map/ppermute | solution.py:100
  288.8 19.0 %collective-permute-done.12 = bf16[128,2,1280]{2,0,1:T(8,128)(2,1)S(1)} collective-permute-done((bf16[128,2,1280]{2,0,1:T(8,128)(2,1)S(1)}, bf16[128,2,1280]{2,0,1:T(8,128)(2,1)S(1)}, u32[]{:S(2)}, u32[]{:S(2)}) %collective-permute-start.12) | collective-permute-done | bytes 655392 | tf_op jit(solution)/shard_map/ppermute | solution.py:100
  308.6 18.0 %collective-permute-done.13 = bf16[128,2,1280]{2,0,1:T(8,128)(2,1)} collective-permute-done((bf16[128,2,1280]{2,0,1:T(8,128)(2,1)S(1)}, bf16[128,2,1280]{2,0,1:T(8,128)(2,1)}, u32[]{:S(2)}, u32[]{:S(2)}) %collective-permute-start.13) | collective-permute-done | bytes 655392 | tf_op jit(solution)/shard_map/ppermute | solution.py:100
  326.7 16.8 %collective-permute-done.14 = bf16[128,2,1280]{2,0,1:T(8,128)(2,1)} collective-permute-done((bf16[128,2,1280]{2,0,1:T(8,128)(2,1)}, bf16[128,2,1280]{2,0,1:T(8,128)(2,1)}, u32[]{:S(2)}, u32[]{:S(2)}) %collective-permute-start.14) | collective-permute-done | bytes 655392 | tf_op jit(solution)/shard_map/ppermute | solution.py:100
  383.5 8.5 %constant_dynamic-slice_fusion = bf16[2048,2,1280]{2,0,1:T(8,128)(2,1)} fusion(bf16[4096,2,1280]{2,0,1:T(8,128)(2,1)} %constant_dynamic-update-slice_fusion, s32[]{:T(128)S(6)} %select_n.59), kind=kLoop, calls=%fused_computation.118 | loop fusion | bytes 20971524 | tf_op jit(solution)/shard_map/jit(_roll_dynamic)/dynamic_slice | solution.py:103
  392.0 9.1 %multiply_convert_fusion = (bf16[2048,2,160]{0,2,1:T(8,128)(2,1)S(1)}, f32[2048,2,160]{0,2,1:T(8,128)}) fusion(bf16[2048,2,1280]{2,0,1:T(8,128)(2,1)} %constant_dynamic-slice_fusion, bf16[2,160,1280]{2,1,0:T(8,128)(2,1)S(1)} %copy-done), kind=kOutput, calls=%fused_computation.30 | convolution fusion | flops 1680998400 | bytes 15237120 | tf_op jit(solution)/shard_map/rld,lhd->rlh/dot_general | solution.py:23
  402.2 5.6 fusion.6
  407.9 8.4 %fusion.9 = bf16[2048,2,160]{0,2,1:T(8,128)(2,1)S(1)} fusion(bf16[2048,2,1280]{2,0,1:T(8,128)(2,1)} %all-gather.2.cloned.1.call-done, bf16[2,160,1280]{2,1,0:T(8,128)(2,1)S(1)} %copy-done.29, f32[2048,2,160]{0,2,1:T(8,128)} %get-tuple-element.189), kind=kOutput, calls=%fused_computation.25 | convolution fusion | flops 1684275200 | bytes 15237120 | tf_op jit(solution)/shard_map/rld,lhd->rlh/dot_general | solution.py:23
  417.4 5.7 fusion.7
  423.0 92.9 %reduce-scatter.3.cloned.1.call-done = bf16[128,2,1280]{2,0,1:T(8,128)(2,1)} async-done(((bf16[2048,2,1280]{2,0,1:T(8,128)(2,1)}), bf16[128,2,1280]{2,0,1:T(8,128)(2,1)}) %reduce-scatter.3.cloned.1.call-update) | async-done | bytes 655376 | tf_op jit(solution)/shard_map/reduce_scatter | solution.py:106
  517.9 6.0 all-to-all-start.1
  524.0 84.2 %reduce-scatter.5.cloned.1.call-done = bf16[128,2,1280]{2,0,1:T(8,128)(2,1)} async-done(((bf16[2048,2,1280]{2,0,1:T(8,128)(2,1)}), bf16[128,2,1280]{2,0,1:T(8,128)(2,1)}) %reduce-scatter.5.cloned.1.call-update) | async-done | bytes 655376 | tf_op jit(solution)/shard_map/reduce_scatter | solution.py:115
  610.2 6.0 all-to-all-start.3
  616.2 112.5 %while.16 = (s32[]{:T(128)}, f32[2,160,1280]{2,1,0:T(8,128)}, f32[2,160,1280]{2,1,0:T(8,128)}, bf16[2048,2,160]{0,2,1:T(8,128)(2,1)}, bf16[2048,2,1280]{2,0,1:T(...) while((s32[]{:T(128)}, f32[2,160,1280]{2,1,0:T(8,128)}, ...), condition=%wide.region_17.18_spmd.clone, body=%wide.region_16.17_spmd.clone.sunk | while | flops 212992000 | bytes 11307173 | solution.py:137
  624.4 4.1 select_add_fusion.3
  631.6 4.1 select_add_fusion.3
  638.7 4.1 select_add_fusion.3
  (229 shorter events, 200.3 us)
Async XLA Ops:
  7.2 384.9 %copy-start = (bf16[2,160,1280]{2,1,0:T(8,128)(2,1)S(1)}, bf16[2,160,1280]{2,1,0:T(8,128)(2,1)}, u32[]{:S(2)}) copy-start(bf16[2,160,1280]{2,1,0:T(8,128)(2,1)} %param.16) | copy-start | bytes 2457604
  7.2 23.3 %copy-start.27 = (bf16[128,1280]{1,0:T(8,128)(2,1)S(1)}, bf16[128,1280]{1,0:T(8,128)(2,1)}, u32[]{:S(2)}) copy-start(bf16[128,1280]{1,0:T(8,128)(2,1)} %param.11) | copy-start | bytes 983044
  21.3 17.7 %all-to-all-start = ((bf16[8,32,1280]{2,1,0:T(8,128)(2,1)}), bf16[8,32,1280]{2,1,0:T(8,128)(2,1)S(1)}, u32[]{:S(2)}, u32[]{:S(2)}) async-start(bf16[8,32,1280]{2,1,0:T(8,128)(2,1)} %broadcast_select_fusion), calls=%async_computation | async-start | bytes 1310720 | tf_op jit(solution)/shard_map/all_to_all | solution.py:92
  39.0 16.0 %all-to-all-start.2 = ((bf16[8,32,1280]{2,1,0:T(8,128)(2,1)}), bf16[8,32,1280]{2,1,0:T(8,128)(2,1)}, u32[]{:S(2)}, u32[]{:S(2)}) async-start(bf16[8,32,1280]{2,1,0:T(8,128)(2,1)} %multiply_convert_fusion.1), calls=%async_computation.3 | async-start | bytes 1310720 | tf_op jit(solution)/shard_map/all_to_all | solution.py:94
  44.0 363.9 %all-gather.2.cloned.1.call-start = ((), (), s32[]{:S(2)}) async-start(), calls=%async_computation.7 | async-start | bytes 11141120 | tf_op jit(solution)/shard_map/all_gather | solution.py:112
  44.0 19.9 %collective-permute-start = (bf16[128,2,1280]{2,0,1:T(8,128)(2,1)S(1)}, bf16[128,2,1280]{2,0,1:T(8,128)(2,1)S(1)}, u32[]{:S(2)}, u32[]{:S(2)}) collective-permute-start(bf16[128,2,1280]{2,0,1:T(8,128)(2,1)S(1)} %bitcast.64), channel_id=1, source_target_pairs={{0,8},{8,16},{16,24},{24,32},{32,40},{40,48},{48,56},{56,64},{64,7... | collective-permute-start | bytes 1966088 | tf_op jit(solution)/shard_map/ppermute | solution.py:100
  57.0 459.0 %reduce-scatter.3.cloned.1.call-start = ((), (), s32[]{:S(2)}) async-start(), calls=%async_computation.6 | async-start | bytes 11141120 | tf_op jit(solution)/shard_map/reduce_scatter | solution.py:106
  63.9 28.0 %collective-permute-start.1 = (bf16[128,2,1280]{2,0,1:T(8,128)(2,1)S(1)}, bf16[128,2,1280]{2,0,1:T(8,128)(2,1)S(1)}, u32[]{:S(2)}, u32[]{:S(2)}) collective-permute-start(bf16[128,2,1280]{2,0,1:T(8,128)(2,1)S(1)} %collective-permute-done), channel_id=1, source_target_pairs={{0,8},{8,16},{16,24},{24,32},{32,40},{40,48},{48,56},{56,64},{64,7... | collective-permute-start | bytes 1966088 | tf_op jit(solution)/shard_map/ppermute | solution.py:100
  91.9 21.0 %collective-permute-start.2 = (bf16[128,2,1280]{2,0,1:T(8,128)(2,1)S(1)}, bf16[128,2,1280]{2,0,1:T(8,128)(2,1)S(1)}, u32[]{:S(2)}, u32[]{:S(2)}) collective-permute-start(bf16[128,2,1280]{2,0,1:T(8,128)(2,1)S(1)} %collective-permute-done.1), channel_id=1, source_target_pairs={{0,8},{8,16},{16,24},{24,32},{32,40},{40,48},{48,56},{56,64},{64,7... | collective-permute-start | bytes 1966088 | tf_op jit(solution)/shard_map/ppermute | solution.py:100
  113.8 31.5 %collective-permute-start.3 = (bf16[128,2,1280]{2,0,1:T(8,128)(2,1)S(1)}, bf16[128,2,1280]{2,0,1:T(8,128)(2,1)S(1)}, u32[]{:S(2)}, u32[]{:S(2)}) collective-permute-start(bf16[128,2,1280]{2,0,1:T(8,128)(2,1)S(1)} %collective-permute-done.2), channel_id=1, source_target_pairs={{0,8},{8,16},{16,24},{24,32},{32,40},{40,48},{48,56},{56,64},{64,7... | collective-permute-start | bytes 1966088 | tf_op jit(solution)/shard_map/ppermute | solution.py:100
  146.1 31.5 %collective-permute-start.4 = (bf16[128,2,1280]{2,0,1:T(8,128)(2,1)S(1)}, bf16[128,2,1280]{2,0,1:T(8,128)(2,1)S(1)}, u32[]{:S(2)}, u32[]{:S(2)}) collective-permute-start(bf16[128,2,1280]{2,0,1:T(8,128)(2,1)S(1)} %collective-permute-done.3), channel_id=1, source_target_pairs={{0,8},{8,16},{16,24},{24,32},{32,40},{40,48},{48,56},{56,64},{64,7... | collective-permute-start | bytes 1966088 | tf_op jit(solution)/shard_map/ppermute | solution.py:100
  178.5 14.6 %collective-permute-start.5 = (bf16[128,2,1280]{2,0,1:T(8,128)(2,1)S(1)}, bf16[128,2,1280]{2,0,1:T(8,128)(2,1)S(1)}, u32[]{:S(2)}, u32[]{:S(2)}) collective-permute-start(bf16[128,2,1280]{2,0,1:T(8,128)(2,1)S(1)} %collective-permute-done.4), channel_id=1, source_target_pairs={{0,8},{8,16},{16,24},{24,32},{32,40},{40,48},{48,56},{56,64},{64,7... | collective-permute-start | bytes 1966088 | tf_op jit(solution)/shard_map/ppermute | solution.py:100
  194.0 13.7 %collective-permute-start.6 = (bf16[128,2,1280]{2,0,1:T(8,128)(2,1)S(1)}, bf16[128,2,1280]{2,0,1:T(8,128)(2,1)S(1)}, u32[]{:S(2)}, u32[]{:S(2)}) collective-permute-start(bf16[128,2,1280]{2,0,1:T(8,128)(2,1)S(1)} %collective-permute-done.5), channel_id=1, source_target_pairs={{0,8},{8,16},{16,24},{24,32},{32,40},{40,48},{48,56},{56,64},{64,7... | collective-permute-start | bytes 1966088 | tf_op jit(solution)/shard_map/ppermute | solution.py:100
  208.5 12.8 %collective-permute-start.7 = (bf16[128,2,1280]{2,0,1:T(8,128)(2,1)S(1)}, bf16[128,2,1280]{2,0,1:T(8,128)(2,1)S(1)}, u32[]{:S(2)}, u32[]{:S(2)}) collective-permute-start(bf16[128,2,1280]{2,0,1:T(8,128)(2,1)S(1)} %collective-permute-done.6), channel_id=1, source_target_pairs={{0,8},{8,16},{16,24},{24,32},{32,40},{40,48},{48,56},{56,64},{64,7... | collective-permute-start | bytes 1966088 | tf_op jit(solution)/shard_map/ppermute | solution.py:100
  222.1 13.4 %collective-permute-start.8 = (bf16[128,2,1280]{2,0,1:T(8,128)(2,1)S(1)}, bf16[128,2,1280]{2,0,1:T(8,128)(2,1)S(1)}, u32[]{:S(2)}, u32[]{:S(2)}) collective-permute-start(bf16[128,2,1280]{2,0,1:T(8,128)(2,1)S(1)} %collective-permute-done.7), channel_id=1, source_target_pairs={{0,8},{8,16},{16,24},{24,32},{32,40},{40,48},{48,56},{56,64},{64,7... | collective-permute-start | bytes 1966088 | tf_op jit(solution)/shard_map/ppermute | solution.py:100
  236.4 14.5 %collective-permute-start.9 = (bf16[128,2,1280]{2,0,1:T(8,128)(2,1)S(1)}, bf16[128,2,1280]{2,0,1:T(8,128)(2,1)S(1)}, u32[]{:S(2)}, u32[]{:S(2)}) collective-permute-start(bf16[128,2,1280]{2,0,1:T(8,128)(2,1)S(1)} %collective-permute-done.8), channel_id=1, source_target_pairs={{0,8},{8,16},{16,24},{24,32},{32,40},{40,48},{48,56},{56,64},{64,7... | collective-permute-start | bytes 1966088 | tf_op jit(solution)/shard_map/ppermute | solution.py:100
  251.7 15.6 %collective-permute-start.10 = (bf16[128,2,1280]{2,0,1:T(8,128)(2,1)S(1)}, bf16[128,2,1280]{2,0,1:T(8,128)(2,1)S(1)}, u32[]{:S(2)}, u32[]{:S(2)}) collective-permute-start(bf16[128,2,1280]{2,0,1:T(8,128)(2,1)S(1)} %collective-permute-done.9), channel_id=1, source_target_pairs={{0,8},{8,16},{16,24},{24,32},{32,40},{40,48},{48,56},{56,64},{64,7... | collective-permute-start | bytes 1966088 | tf_op jit(solution)/shard_map/ppermute | solution.py:100
  268.1 19.8 %collective-permute-start.11 = (bf16[128,2,1280]{2,0,1:T(8,128)(2,1)S(1)}, bf16[128,2,1280]{2,0,1:T(8,128)(2,1)S(1)}, u32[]{:S(2)}, u32[]{:S(2)}) collective-permute-start(bf16[128,2,1280]{2,0,1:T(8,128)(2,1)S(1)} %collective-permute-done.10), channel_id=1, source_target_pairs={{0,8},{8,16},{16,24},{24,32},{32,40},{40,48},{48,56},{56,64},{64,7... | collective-permute-start | bytes 1966088 | tf_op jit(solution)/shard_map/ppermute | solution.py:100
  288.8 19.0 %collective-permute-start.12 = (bf16[128,2,1280]{2,0,1:T(8,128)(2,1)S(1)}, bf16[128,2,1280]{2,0,1:T(8,128)(2,1)S(1)}, u32[]{:S(2)}, u32[]{:S(2)}) collective-permute-start(bf16[128,2,1280]{2,0,1:T(8,128)(2,1)S(1)} %collective-permute-done.11), channel_id=1, source_target_pairs={{0,8},{8,16},{16,24},{24,32},{32,40},{40,48},{48,56},{56,64},{64,7... | collective-permute-start | bytes 1966088 | tf_op jit(solution)/shard_map/ppermute | solution.py:100
  308.6 18.0 %collective-permute-start.13 = (bf16[128,2,1280]{2,0,1:T(8,128)(2,1)S(1)}, bf16[128,2,1280]{2,0,1:T(8,128)(2,1)}, u32[]{:S(2)}, u32[]{:S(2)}) collective-permute-start(bf16[128,2,1280]{2,0,1:T(8,128)(2,1)S(1)} %collective-permute-done.12), channel_id=1, source_target_pairs={{0,8},{8,16},{16,24},{24,32},{32,40},{40,48},{48,56},{56,64},{64,7... | collective-permute-start | bytes 1966088 | tf_op jit(solution)/shard_map/ppermute | solution.py:100
  326.6 16.8 %collective-permute-start.14 = (bf16[128,2,1280]{2,0,1:T(8,128)(2,1)}, bf16[128,2,1280]{2,0,1:T(8,128)(2,1)}, u32[]{:S(2)}, u32[]{:S(2)}) collective-permute-start(bf16[128,2,1280]{2,0,1:T(8,128)(2,1)} %collective-permute-done.13), channel_id=1, source_target_pairs={{0,8},{8,16},{16,24},{24,32},{32,40},{40,48},{48,56},{56,64},{64,7... | collective-permute-start | bytes 1966088 | tf_op jit(solution)/shard_map/ppermute | solution.py:100
  326.6 33.1 %copy-start.13 = (bf16[128,2,1280]{2,0,1:T(8,128)(2,1)S(1)}, bf16[128,2,1280]{2,0,1:T(8,128)(2,1)}, u32[]{:S(2)}) copy-start(bf16[128,2,1280]{2,0,1:T(8,128)(2,1)} %copy-done.12) | copy-start | bytes 1966084
  326.6 34.0 %copy-start.11 = (bf16[128,2,1280]{2,0,1:T(8,128)(2,1)S(1)}, bf16[128,2,1280]{2,0,1:T(8,128)(2,1)}, u32[]{:S(2)}) copy-start(bf16[128,2,1280]{2,0,1:T(8,128)(2,1)} %copy-done.10) | copy-start | bytes 1966084
  326.6 34.9 %copy-start.9 = (bf16[128,2,1280]{2,0,1:T(8,128)(2,1)S(1)}, bf16[128,2,1280]{2,0,1:T(8,128)(2,1)}, u32[]{:S(2)}) copy-start(bf16[128,2,1280]{2,0,1:T(8,128)(2,1)} %copy-done.8) | copy-start | bytes 1966084
  326.6 35.8 %copy-start.7 = (bf16[128,2,1280]{2,0,1:T(8,128)(2,1)S(1)}, bf16[128,2,1280]{2,0,1:T(8,128)(2,1)}, u32[]{:S(2)}) copy-start(bf16[128,2,1280]{2,0,1:T(8,128)(2,1)} %copy-done.6) | copy-start | bytes 1966084
  326.6 36.7 %copy-start.5 = (bf16[128,2,1280]{2,0,1:T(8,128)(2,1)S(1)}, bf16[128,2,1280]{2,0,1:T(8,128)(2,1)}, u32[]{:S(2)}) copy-start(bf16[128,2,1280]{2,0,1:T(8,128)(2,1)} %copy-done.4) | copy-start | bytes 1966084
  347.4 23.5 %copy-start.25 = (bf16[128,2,1280]{2,0,1:T(8,128)(2,1)S(1)}, bf16[128,2,1280]{2,0,1:T(8,128)(2,1)}, u32[]{:S(2)}) copy-start(bf16[128,2,1280]{2,0,1:T(8,128)(2,1)} %copy-done.24) | copy-start | bytes 1966084
  349.4 22.3 %copy-start.23 = (bf16[128,2,1280]{2,0,1:T(8,128)(2,1)S(1)}, bf16[128,2,1280]{2,0,1:T(8,128)(2,1)}, u32[]{:S(2)}) copy-start(bf16[128,2,1280]{2,0,1:T(8,128)(2,1)} %copy-done.22) | copy-start | bytes 1966084
  351.5 21.2 %copy-start.21 = (bf16[128,2,1280]{2,0,1:T(8,128)(2,1)S(1)}, bf16[128,2,1280]{2,0,1:T(8,128)(2,1)}, u32[]{:S(2)}) copy-start(bf16[128,2,1280]{2,0,1:T(8,128)(2,1)} %copy-done.20) | copy-start | bytes 1966084
  407.8 200.4 %reduce-scatter.5.cloned.1.call-start = ((), (), s32[]{:S(2)}) async-start(), calls=%async_computation.8 | async-start | bytes 11141120 | tf_op jit(solution)/shard_map/reduce_scatter | solution.py:115
  517.9 92.3 %all-to-all-start.1 = ((bf16[8,32,1280]{2,1,0:T(8,128)(2,1)}), bf16[8,32,1280]{2,1,0:T(8,128)(2,1)S(1)}, u32[]{:S(2)}, u32[]{:S(2)}) async-start(bf16[8,32,1280]{2,1,0:T(8,128)(2,1)} %bitcast.13), calls=%async_computation.2 | async-start | bytes 1310720 | tf_op jit(solution)/shard_map/all_to_all | solution.py:142
  610.2 133.0 %all-to-all-start.3 = ((bf16[8,32,1280]{2,1,0:T(8,128)(2,1)}), bf16[8,32,1280]{2,1,0:T(8,128)(2,1)}, u32[]{:S(2)}, u32[]{:S(2)}) async-start(bf16[8,32,1280]{2,1,0:T(8,128)(2,1)} %bitcast.23), calls=%async_computation.5 | async-start | bytes 1310720 | tf_op jit(solution)/shard_map/all_to_all | solution.py:152
  (21 other events, 136.4 us)
Sparse Core Ops, SparseCore 0:
  57.1 121.5 all-gather.1
  407.9 107.9 reduce-scatter.2
  519.4 88.7 reduce-scatter.4
